TPU v7x, 32 devices: a whole 2x2x4 slice. The times are simulated.
32 devices in a mesh: ctx: 4 (over z), head: 8 (over y, x, core).
Axes of the slice: x: 2, y: 2, z: 4, core: 2. Of those that a mesh axis runs over, the one named last changes fastest.
Arguments:
- queries: bfloat16 [4096, 4096], P(('ctx', 'head')), may hold values from -12 to 12
- keys_in: bfloat16 [4096, 4096], P(('ctx', 'head')), may hold values from -5 to 5
- values_in: bfloat16 [4096, 4096], P(('ctx', 'head')), may hold values from -6 to 6
- out_grad: bfloat16 [4096, 4096], P(('ctx', 'head')), may hold values from -6 to 6
- rand_owner: int32 [32, 3], replicated, may hold values from 0 to 3, all different within a row; in each aligned block of 8 rows (0 to 7, 8 to 15, ...) at most 8 rows name the same one
- rand_local: int32 [32, 3], replicated, may hold values from 0 to 7
Outputs:
- grad_queries: bfloat16 [4096, 4096], P(('ctx', 'head'))
- grad_keys: bfloat16 [4096, 4096], P(('ctx', 'head'))
- grad_values: bfloat16 [4096, 4096], P(('ctx', 'head'))
Inputs may be any that keep to these rules, and one draw needn't show every extreme that they name: `rand_owner`: each row names 3 different ranges. Among the 8 rows of one aligned block of rows, at most 8 name the same range.
All inputs are finite; a program needn't handle non-finite values.
Results may differ from a plain program's by a relative error of at most 0.035.
Values may be sent and summed in bfloat16 or wider, within the bound.
A program may use at most 192 MiB of HBM per device.

v0:
```python
import functools
import math

import jax
import jax.numpy as jnp
from jax import lax
from jax.experimental import pallas as pl
from jax.experimental.pallas import tpu as pltpu
from jax.sharding import PartitionSpec as P

MESH = pl.DeviceIdType.MESH

HEAD_DIM = 128
BLOCK_LEN = 128
GLOBALS = 2


NEG_BIG = -1e30


def broadcast(block, axis, holder):
    block = jnp.where(lax.axis_index(axis) == holder, block, jnp.zeros_like(block))
    return lax.psum(block, axis)


def entry_blocks(rand_owner, rand_local, range_blocks, glob_count, total_blocks):
    block_ids = jnp.arange(total_blocks, dtype=jnp.int32)
    fixed_cols = [block_ids - 1, block_ids, block_ids + 1]
    fixed_cols = fixed_cols + [
        jnp.full((total_blocks,), glob_id, jnp.int32) for glob_id in range(glob_count)
    ]
    listed = jnp.concatenate(
        [jnp.stack(fixed_cols, axis=1), rand_owner * range_blocks + rand_local], axis=1
    )
    inside = (listed >= 0) & (listed < total_blocks)
    entry_count = listed.shape[1]
    equal_pair = (listed[:, :, None] == listed[:, None, :]) & inside[:, None, :]
    earlier = jnp.tril(jnp.ones((entry_count, entry_count), jnp.int32), -1) > 0
    repeated = jnp.any(equal_pair & earlier[None, :, :], axis=2)
    usable = inside & jnp.logical_not(repeated) & (block_ids >= glob_count)[:, None]
    return (jnp.clip(listed, 0, total_blocks - 1), usable)


def head_major(rows_arr, block_len, head_dim):
    row_count, feat_width = rows_arr.shape
    shaped = rows_arr.reshape(row_count // block_len, block_len, feat_width // head_dim, head_dim)
    return jnp.transpose(shaped, (0, 2, 1, 3))


def token_major(blocks_arr):
    block_count, heads, block_len, head_dim = blocks_arr.shape
    return jnp.transpose(blocks_arr, (0, 2, 1, 3)).reshape(
        block_count * block_len, heads * head_dim
    )


def regular_part(q_blocks, g_blocks, key_pool, pool_index, usable, score_scale):
    range_blocks, local_heads, block_len, head_dim = q_blocks.shape
    entry_count = pool_index.shape[1]
    group_size = math.gcd(range_blocks, max(1, 512 // block_len))
    group_count = range_blocks // group_size

    def split_groups(tensor):
        return tensor.reshape((group_count, group_size) + tensor.shape[1:])

    def group_step(grad_acc, inputs):
        q_tile, g_tile, index_group, usable_group = inputs
        kv_tile = jnp.stack(
            [
                lax.dynamic_index_in_dim(key_pool, index_group[row, col], 0, keepdims=False)
                for row in range(group_size)
                for col in range(entry_count)
            ]
        ).reshape(index_group.shape + key_pool.shape[1:])
        k_tile = kv_tile[:, :, 0]
        v_tile = kv_tile[:, :, 1]
        key_mask = usable_group[:, None, None, :, None]
        scores = (
            jnp.einsum("ghqd,gehkd->ghqek", q_tile, k_tile, preferred_element_type=jnp.float32)
            * score_scale
        )
        scores = jnp.where(key_mask, scores, NEG_BIG)
        row_top = jnp.max(scores, axis=(3, 4), keepdims=True)
        row_total = jnp.sum(
            jnp.where(key_mask, jnp.exp(scores - row_top), 0.0), axis=(3, 4), keepdims=True
        )
        log_norm = row_top + jnp.log(jnp.where(row_total > 0, row_total, 1.0))
        prob_vals = jnp.where(key_mask, jnp.exp(scores - log_norm), 0.0)
        probs_bf = prob_vals.astype(jnp.bfloat16)
        attended = jnp.einsum(
            "ghqek,gehkd->ghqd", probs_bf, v_tile, preferred_element_type=jnp.float32
        )
        row_delta = jnp.sum(g_tile.astype(jnp.float32) * attended, axis=3)
        dprobs = jnp.einsum("ghqd,gehkd->ghqek", g_tile, v_tile, preferred_element_type=jnp.float32)
        dscores = prob_vals * (dprobs - row_delta[:, :, :, None, None])
        ds_bf = dscores.astype(jnp.bfloat16)
        dq_tile = (
            jnp.einsum("ghqek,gehkd->ghqd", ds_bf, k_tile, preferred_element_type=jnp.float32)
            * score_scale
        ).astype(jnp.bfloat16)
        dk_tile = (
            jnp.einsum("ghqek,ghqd->gehkd", ds_bf, q_tile, preferred_element_type=jnp.float32)
            * score_scale
        )
        dv_tile = jnp.einsum(
            "ghqek,ghqd->gehkd", probs_bf, g_tile, preferred_element_type=jnp.float32
        )
        grads = jnp.stack([dk_tile, dv_tile], axis=2)
        grads = grads.reshape((group_size * entry_count,) + grads.shape[2:])
        grad_acc = grad_acc.at[index_group.reshape(-1)].add(grads)
        return (grad_acc, dq_tile)

    zero_acc = jnp.zeros(key_pool.shape, jnp.float32)
    inputs = (
        split_groups(q_blocks),
        split_groups(g_blocks),
        split_groups(pool_index),
        split_groups(usable),
    )
    grad_acc, dq_groups = lax.scan(group_step, zero_acc, inputs)
    return (grad_acc, dq_groups.reshape(q_blocks.shape))


def global_scores(q_glob, k_slice, score_scale):
    return (
        jnp.einsum("hqd,nhbd->hqnb", q_glob, k_slice, preferred_element_type=jnp.float32)
        * score_scale
    )


def global_grads(scores, log_norm, row_delta, g_glob, v_slice):
    prob_vals = jnp.exp(scores - log_norm[:, :, None, None])
    probs_bf = prob_vals.astype(jnp.bfloat16)
    dprobs = jnp.einsum("hqd,nhbd->hqnb", g_glob, v_slice, preferred_element_type=jnp.float32)
    ds_bf = (prob_vals * (dprobs - row_delta[:, :, None, None])).astype(jnp.bfloat16)
    return (probs_bf, ds_bf)


def split_heads(queries, keys_in, values_in, out_grad, rand_owner, rand_local):
    q_local, k_local, v_local, g_local = (
        lax.all_to_all(queries, "head", split_axis=1, concat_axis=0, tiled=True),
        lax.all_to_all(keys_in, "head", split_axis=1, concat_axis=0, tiled=True),
        lax.all_to_all(values_in, "head", split_axis=1, concat_axis=0, tiled=True),
        lax.all_to_all(out_grad, "head", split_axis=1, concat_axis=0, tiled=True),
    )
    n_ctx = lax.axis_size("ctx")
    ctx_id = lax.axis_index("ctx")
    local_rows, feat_width = q_local.shape
    range_blocks = local_rows // BLOCK_LEN
    local_heads = feat_width // HEAD_DIM
    total_blocks = range_blocks * n_ctx
    glob_rows = GLOBALS * BLOCK_LEN
    score_scale = 1.0 / math.sqrt(HEAD_DIM)
    q_blocks = head_major(q_local, BLOCK_LEN, HEAD_DIM)
    g_blocks = head_major(g_local, BLOCK_LEN, HEAD_DIM)
    kv_local = jnp.stack(
        [head_major(k_local, BLOCK_LEN, HEAD_DIM), head_major(v_local, BLOCK_LEN, HEAD_DIM)], axis=1
    )
    pool_tail = (2, local_heads, BLOCK_LEN, HEAD_DIM)
    listed, usable = entry_blocks(rand_owner, rand_local, range_blocks, GLOBALS, total_blocks)
    my_listed = lax.dynamic_slice_in_dim(listed, ctx_id * range_blocks, range_blocks, 0)
    my_usable = lax.dynamic_slice_in_dim(usable, ctx_id * range_blocks, range_blocks, 0)
    key_pool = lax.all_gather(kv_local, "ctx", axis=0, tiled=True)
    grad_acc, dq_regular = regular_part(
        q_blocks, g_blocks, key_pool, my_listed, my_usable, score_scale
    )
    summed = lax.psum_scatter(
        grad_acc.astype(jnp.bfloat16), "ctx", scatter_dimension=0, tiled=True
    ).astype(jnp.float32)
    q_shared, g_shared = (
        broadcast(q_blocks[:GLOBALS], "ctx", 0),
        broadcast(g_blocks[:GLOBALS], "ctx", 0),
    )
    q_glob = jnp.transpose(q_shared, (1, 0, 2, 3)).reshape(local_heads, glob_rows, HEAD_DIM)
    g_glob = jnp.transpose(g_shared, (1, 0, 2, 3)).reshape(local_heads, glob_rows, HEAD_DIM)
    k_own = kv_local[:, 0]
    v_own = kv_local[:, 1]
    slice_parts = key_pool.reshape((n_ctx, range_blocks) + pool_tail)

    def stats_step(stats_carry, slice_part):
        row_top, row_total = stats_carry
        scores = global_scores(q_glob, slice_part[:, 0], score_scale)
        new_top = jnp.maximum(row_top, jnp.max(scores, axis=(2, 3)))
        row_total = row_total * jnp.exp(row_top - new_top) + jnp.sum(
            jnp.exp(scores - new_top[:, :, None, None]), axis=(2, 3)
        )
        return ((new_top, row_total), None)

    start_stats = (
        jnp.full((local_heads, glob_rows), NEG_BIG, jnp.float32),
        jnp.zeros((local_heads, glob_rows), jnp.float32),
    )
    (row_top, row_total), _ = lax.scan(stats_step, start_stats, slice_parts)
    log_norm = row_top + jnp.log(row_total)

    def out_step(attended, slice_part):
        scores = global_scores(q_glob, slice_part[:, 0], score_scale)
        probs_bf = jnp.exp(scores - log_norm[:, :, None, None]).astype(jnp.bfloat16)
        return (
            attended
            + jnp.einsum(
                "hqnb,nhbd->hqd", probs_bf, slice_part[:, 1], preferred_element_type=jnp.float32
            ),
            None,
        )

    attended, _ = lax.scan(
        out_step, jnp.zeros((local_heads, glob_rows, HEAD_DIM), jnp.float32), slice_parts
    )
    row_delta = jnp.sum(g_glob.astype(jnp.float32) * attended, axis=2)

    def dq_step(dq_acc, slice_part):
        k_slice = slice_part[:, 0]
        scores = global_scores(q_glob, k_slice, score_scale)
        probs_bf, ds_bf = global_grads(scores, log_norm, row_delta, g_glob, slice_part[:, 1])
        return (
            dq_acc
            + jnp.einsum("hqnb,nhbd->hqd", ds_bf, k_slice, preferred_element_type=jnp.float32)
            * score_scale,
            None,
        )

    dq_glob, _ = lax.scan(
        dq_step, jnp.zeros((local_heads, glob_rows, HEAD_DIM), jnp.float32), slice_parts
    )
    own_scores = global_scores(q_glob, k_own, score_scale)
    probs_bf, ds_bf = global_grads(own_scores, log_norm, row_delta, g_glob, v_own)
    dk_glob = (
        jnp.einsum("hqnb,hqd->nhbd", ds_bf, q_glob, preferred_element_type=jnp.float32)
        * score_scale
    )
    dv_glob = jnp.einsum("hqnb,hqd->nhbd", probs_bf, g_glob, preferred_element_type=jnp.float32)
    glob_extra = jnp.stack([dk_glob, dv_glob], axis=1)
    final_kv = (summed + glob_extra).astype(jnp.bfloat16)
    dq_rows = token_major(dq_regular)
    glob_dq_rows = (
        jnp.transpose(dq_glob, (1, 0, 2)).reshape(glob_rows, feat_width).astype(jnp.bfloat16)
    )
    head_rows = jnp.where(ctx_id == 0, glob_dq_rows, dq_rows[:glob_rows])
    dq_final = jnp.concatenate([head_rows, dq_rows[glob_rows:]], axis=0)
    dk_final = token_major(final_kv[:, 0])
    dv_final = token_major(final_kv[:, 1])
    return (
        lax.all_to_all(dq_final, "head", split_axis=0, concat_axis=1, tiled=True),
        lax.all_to_all(dk_final, "head", split_axis=0, concat_axis=1, tiled=True),
        lax.all_to_all(dv_final, "head", split_axis=0, concat_axis=1, tiled=True),
    )


def dot_nn(left, right):
    return lax.dot_general(left, right, (((1,), (0,)), ((), ())), preferred_element_type=jnp.float32)


def dot_nt(left, right):
    return lax.dot_general(left, right, (((1,), (1,)), ((), ())), preferred_element_type=jnp.float32)


def links_kernel(
    range_blocks, owner_ref, local_ref, named_ref, bias_ref, prev_ref, has_prev_ref, last_ref, has_last_ref
):
    blocks, randoms = owner_ref.shape

    def clear(block_id, carry):
        last_ref[block_id] = 0
        has_last_ref[block_id] = 0.0
        return carry

    lax.fori_loop(0, blocks, clear, 0)

    def link(block_id, carry):
        earlier = []
        for nth in range(randoms):
            named = owner_ref[block_id, nth] * range_blocks + local_ref[block_id, nth]
            fresh = (named >= GLOBALS) & ((named < block_id - 1) | (named > block_id + 1))
            for before in earlier:
                fresh = fresh & (named != before)
            earlier.append(named)
            edge = block_id * randoms + nth
            named_ref[edge] = named
            bias_ref[edge] = jnp.where(fresh, 0.0, -NEG_BIG).astype(jnp.float32)
            prev_ref[edge] = last_ref[named]
            has_prev_ref[edge] = has_last_ref[named]

            @pl.when(block_id >= GLOBALS)
            def _():
                last_ref[named] = edge
                has_last_ref[named] = 1.0

        return carry

    lax.fori_loop(0, blocks, link, 0)


def head_kernel(ctx_size, heads_axis, named_ref, bias_ref, prev_ref, has_prev_ref, last_ref, has_last_ref,
                k_in, v_in, q_in, g_in, dq_out, dk_out, dv_out,
                kv_ref, qg_ref, grads_ref, acc_ref, edge_ref, kt_ref, pair_ref, s_ref, dp_ref,
                send_sem, recv_sem, own_sem):
    blocks, randoms = kv_ref.shape[0], edge_ref.shape[0] // kv_ref.shape[0]
    devices = ctx_size * heads_axis
    score_scale = 1.0 / math.sqrt(HEAD_DIM)
    exp_scale = score_scale * math.log2(math.e)
    glob_rows = GLOBALS * BLOCK_LEN
    group = 4
    chunk = group * BLOCK_LEN
    chunks = blocks // group
    bf16 = jnp.bfloat16
    ctx_id, head_id = lax.axis_index("ctx"), lax.axis_index("head")
    me = ctx_id * heads_axis + head_id
    own_step = ctx_size - 1
    ins = (k_in, v_in, q_in, g_in)
    landing = (kv_ref, kv_ref, qg_ref, qg_ref)
    outs = (dq_out, dk_out, dv_out)

    def head_columns(block_id):
        return pl.ds(pl.multiple_of(block_id * HEAD_DIM, HEAD_DIM), HEAD_DIM)

    def peer_at(step):
        ctx_off, head_off = ctx_size - 1 - step % ctx_size, step // ctx_size
        return ctx_id ^ ctx_off, head_id ^ head_off, ctx_off * heads_axis + head_off

    def ends(which, peer):
        if which < 4:
            half = (which % 2) * HEAD_DIM
            return (
                ins[which].at[:, head_columns(peer)],
                landing[which].at[me, :, half : half + HEAD_DIM],
            )
        return (
            grads_ref.at[which - 4, peer],
            outs[which - 4].at[:, head_columns(me)],
        )

    def remote(which, peer_ctx, peer_head, offset):
        src, dst = ends(which, peer_ctx * heads_axis + peer_head)
        return pltpu.make_async_remote_copy(
            src_ref=src,
            dst_ref=dst,
            send_sem=send_sem.at[which, offset],
            recv_sem=recv_sem.at[which, offset],
            device_id=(peer_ctx, peer_head),
            device_id_type=MESH,
        )

    def own(which):
        src, dst = ends(which, me)
        return pltpu.make_async_copy(src, dst, own_sem.at[which])

    def over_peers(action):
        def one(step, carry):
            @pl.when(step != own_step)
            def _():
                action(*peer_at(step))

            return carry

        lax.fori_loop(0, devices, one, 0)

    def start_all(*names):
        def action(*peer):
            for which in names:
                remote(which, *peer).start()

        over_peers(action)

    barrier = pltpu.get_barrier_semaphore()

    def greet(peer_ctx, peer_head, offset):
        pl.semaphore_signal(barrier, inc=1, device_id=(peer_ctx, peer_head), device_id_type=MESH)

    over_peers(greet)
    pl.semaphore_wait(barrier, devices - 1)
    start_all(0)
    start_all(1)
    start_all(2, 3)
    for which in range(4):
        own(which).start()
    pair_ref[...] = jnp.zeros_like(pair_ref)
    acc_ref[...] = jnp.zeros_like(acc_ref)
    edge_ref[: GLOBALS * randoms] = jnp.zeros(
        (GLOBALS * randoms, BLOCK_LEN, 2 * HEAD_DIM), jnp.float32
    )
    for which in range(4):
        own(which).wait()

    def keys_arrived(*peer):
        remote(0, *peer).wait_recv()
        remote(1, *peer).wait_recv()

    over_peers(keys_arrived)

    def turn_step(block_id, carry):
        kt_ref[block_id] = kv_ref[block_id, :, :HEAD_DIM].T
        return carry

    lax.fori_loop(0, blocks, turn_step, 0, unroll=4)

    def attend(block_id):
        pair_ref[:BLOCK_LEN, :HEAD_DIM] = qg_ref[block_id, :, :HEAD_DIM]
        pair_ref[BLOCK_LEN:, HEAD_DIM:] = qg_ref[block_id, :, HEAD_DIM:]
        pair = pair_ref[...]
        ids = [block_id - 1, block_id, jnp.minimum(block_id + 1, blocks - 1)]
        bias = [
            jnp.where(block_id - 1 >= GLOBALS, 0.0, -NEG_BIG).astype(jnp.float32),
            0.0,
            jnp.where(block_id + 1 < blocks, 0.0, -NEG_BIG).astype(jnp.float32),
        ]
        ids += list(range(GLOBALS))
        bias += [0.0] * GLOBALS
        fixed = len(ids)
        for nth in range(randoms):
            ids.append(named_ref[block_id * randoms + nth])
            bias.append(bias_ref[block_id * randoms + nth])
        both = [dot_nt(kv_ref[key_id], pair) for key_id in ids]
        row_top = None
        for part, off in zip(both, bias):
            part_top = jnp.max(part[:, :BLOCK_LEN], axis=0, keepdims=True) - off
            row_top = part_top if row_top is None else jnp.maximum(row_top, part_top)
        top_scaled = row_top * exp_scale
        probs, row_total, row_dot = [], 0.0, 0.0
        for part, off in zip(both, bias):
            vals = jnp.exp2(part[:, :BLOCK_LEN] * exp_scale - (top_scaled + off))
            row_total += jnp.sum(vals, axis=0, keepdims=True)
            row_dot += jnp.sum(vals * part[:, BLOCK_LEN:], axis=0, keepdims=True)
            probs.append(vals)
        inverse = 1.0 / row_total
        row_delta = row_dot * inverse
        dq_acc = jnp.zeros((HEAD_DIM, BLOCK_LEN), jnp.float32)
        for nth, (part, vals, key_id) in enumerate(zip(both, probs, ids)):
            vals = vals * inverse
            ds_bf = (vals * (part[:, BLOCK_LEN:] - row_delta)).astype(bf16)
            left = jnp.concatenate([ds_bf, vals.astype(bf16)], axis=1)
            if nth < fixed:
                acc_ref[key_id] += dot_nn(left, pair)
            else:
                edge_ref[block_id * randoms + nth - fixed] = dot_nn(left, pair)
            dq_acc += dot_nn(kt_ref[key_id], ds_bf)
        grads_ref[0, block_id] = (dq_acc.T * score_scale).astype(bf16)

    def block_step(step, carry):
        peer = peer_at(step)
        block_id = peer[0] * heads_axis + peer[1]

        @pl.when(step != own_step)
        def _():
            remote(2, *peer).wait_recv()
            remote(3, *peer).wait_recv()

        @pl.when(block_id >= GLOBALS)
        def _():
            attend(block_id)

            @pl.when(step != own_step)
            def _():
                remote(4, *peer).start()

        return carry

    lax.fori_loop(0, devices, block_step, 0)

    q_glob = qg_ref[:GLOBALS, :, :HEAD_DIM].reshape(glob_rows, HEAD_DIM)
    g_glob = qg_ref[:GLOBALS, :, HEAD_DIM:].reshape(glob_rows, HEAD_DIM)

    def keys_of(step, half):
        part = kv_ref[pl.ds(step * group, group), :, half * HEAD_DIM : (half + 1) * HEAD_DIM]
        return part.reshape(chunk, HEAD_DIM)

    def scores_step(step, row_top):
        rows = pl.ds(pl.multiple_of(step * chunk, chunk), chunk)
        scores = dot_nt(keys_of(step, 0), q_glob)
        s_ref[rows, :] = scores
        return jnp.maximum(row_top, jnp.max(scores, axis=0, keepdims=True))

    row_top = lax.fori_loop(
        0, chunks, scores_step, jnp.full((1, glob_rows), NEG_BIG, jnp.float32)
    )
    top_scaled = row_top * exp_scale

    def probs_step(step, sums):
        rows = pl.ds(pl.multiple_of(step * chunk, chunk), chunk)
        probs = jnp.exp2(s_ref[rows, :] * exp_scale - top_scaled)
        dprobs = dot_nt(keys_of(step, 1), g_glob)
        s_ref[rows, :] = probs
        dp_ref[rows, :] = dprobs
        return (
            sums[0] + jnp.sum(probs, axis=0, keepdims=True),
            sums[1] + jnp.sum(probs * dprobs, axis=0, keepdims=True),
        )

    zero_row = jnp.zeros((1, glob_rows), jnp.float32)
    row_total, row_dot = lax.fori_loop(0, chunks, probs_step, (zero_row, zero_row))
    inverse = 1.0 / row_total
    row_delta = row_dot * inverse

    def grads_step(step, dq_acc):
        rows = pl.ds(pl.multiple_of(step * chunk, chunk), chunk)
        probs = s_ref[rows, :] * inverse
        ds_bf = (probs * (dp_ref[rows, :] - row_delta)).astype(bf16)
        probs_bf = probs.astype(bf16)
        at = pl.ds(step * group, group)
        shape = (group, BLOCK_LEN, HEAD_DIM)
        acc_ref[at, :, :HEAD_DIM] += dot_nn(ds_bf, q_glob).reshape(shape)
        acc_ref[at, :, HEAD_DIM:] += dot_nn(probs_bf, g_glob).reshape(shape)
        for nth in range(group):
            dq_acc += dot_nn(
                kt_ref[step * group + nth], ds_bf[nth * BLOCK_LEN : (nth + 1) * BLOCK_LEN]
            )
        return dq_acc

    dq_glob = lax.fori_loop(
        0, chunks, grads_step, jnp.zeros((HEAD_DIM, glob_rows), jnp.float32)
    )
    dq_rows = (dq_glob.T * score_scale).astype(bf16)
    for block_id in range(GLOBALS):
        grads_ref[0, block_id] = dq_rows[block_id * BLOCK_LEN : (block_id + 1) * BLOCK_LEN]

        @pl.when(me != block_id)
        def _():
            remote(4, 0, block_id, ctx_id * heads_axis + (head_id ^ block_id)).start()

    own(4).start()

    def chain_step(edge, carry):
        edge_ref[edge] += has_prev_ref[edge] * edge_ref[prev_ref[edge]]
        return carry

    lax.fori_loop(GLOBALS * randoms, blocks * randoms, chain_step, 0)

    def finish_step(step, carry):
        peer = peer_at(step)
        block_id = peer[0] * heads_axis + peer[1]
        total = acc_ref[block_id] + has_last_ref[block_id] * edge_ref[last_ref[block_id]]
        grads_ref[1, block_id] = (total[:, :HEAD_DIM] * score_scale).astype(bf16)
        grads_ref[2, block_id] = total[:, HEAD_DIM:].astype(bf16)

        @pl.when(step != own_step)
        def _():
            remote(5, *peer).start()
            remote(6, *peer).start()

        return carry

    lax.fori_loop(0, devices, finish_step, 0)
    own(5).start()
    own(6).start()
    for which in range(4, 7):
        own(which).wait()

    def all_done(*peer):
        for which in range(4):
            remote(which, *peer).wait_send()
        for which in range(4, 7):
            remote(which, *peer).wait()

    over_peers(all_done)


def one_head(queries, keys_in, values_in, out_grad, rand_owner, rand_local):
    ctx_size, heads_axis = lax.axis_size("ctx"), lax.axis_size("head")
    devices = ctx_size * heads_axis
    rows, feat_width = queries.shape
    tokens = rows * devices
    blocks, randoms = rand_owner.shape
    edges = blocks * randoms
    anywhere = pl.BlockSpec(memory_space=pl.ANY)
    smem = pl.BlockSpec(memory_space=pltpu.SMEM)
    bf16 = jnp.bfloat16
    tables = pl.pallas_call(
        functools.partial(links_kernel, blocks // ctx_size),
        out_shape=[
            jax.ShapeDtypeStruct((count,), kind)
            for count in (edges, edges, blocks)
            for kind in (jnp.int32, jnp.float32)
        ],
        in_specs=[smem] * 2,
        out_specs=[smem] * 6,
    )(rand_owner, rand_local)
    return tuple(
        pl.pallas_call(
            functools.partial(head_kernel, ctx_size, heads_axis),
            out_shape=[jax.ShapeDtypeStruct((rows, feat_width), bf16)] * 3,
            in_specs=[smem] * 6 + [anywhere] * 4,
            out_specs=[anywhere] * 3,
            scratch_shapes=[
                pltpu.VMEM((blocks, BLOCK_LEN, 2 * HEAD_DIM), bf16),
                pltpu.VMEM((blocks, BLOCK_LEN, 2 * HEAD_DIM), bf16),
                pltpu.VMEM((3, blocks, BLOCK_LEN, HEAD_DIM), bf16),
                pltpu.VMEM((blocks, BLOCK_LEN, 2 * HEAD_DIM), jnp.float32),
                pltpu.VMEM((edges, BLOCK_LEN, 2 * HEAD_DIM), jnp.float32),
                pltpu.VMEM((blocks, HEAD_DIM, BLOCK_LEN), bf16),
                pltpu.VMEM((2 * BLOCK_LEN, 2 * HEAD_DIM), bf16),
                pltpu.VMEM((tokens, GLOBALS * BLOCK_LEN), jnp.float32),
                pltpu.VMEM((tokens, GLOBALS * BLOCK_LEN), jnp.float32),
                pltpu.SemaphoreType.DMA((7, devices)),
                pltpu.SemaphoreType.DMA((7, devices)),
                pltpu.SemaphoreType.DMA((7,)),
            ],
            compiler_params=pltpu.CompilerParams(
                collective_id=1, has_side_effects=True, vmem_limit_bytes=52 << 20
            ),
        )(
            *tables,
            keys_in,
            values_in,
            queries,
            out_grad,
        )
    )


def per_device(*args):
    devices = lax.axis_size(("ctx", "head"))
    rows, feat_width = args[0].shape
    fits = feat_width == devices * HEAD_DIM and rows == BLOCK_LEN and devices % 4 == 0
    return one_head(*args) if fits else split_heads(*args)


def solution(mesh):
    return jax.shard_map(
        per_device,
        mesh=mesh,
        in_specs=(
            P(("ctx", "head"), None),
            P(("ctx", "head"), None),
            P(("ctx", "head"), None),
            P(("ctx", "head"), None),
            P(),
            P(),
        ),
        out_specs=(P(("ctx", "head"), None), P(("ctx", "head"), None), P(("ctx", "head"), None)),
        check_vma=False,
    )
```

profile of v0, /device:TPU:0, one launch (start us, length us, event | category | flops | bytes accessed | tf_op | source)
XLA Modules:
  0.0 189.4 jit_solution(2885501487515677712)
XLA Ops:
  0.6 0.0 copy-start.8
  0.6 1.4 copy.9.owner_ref
  2.0 0.0 copy-done.8
  2.0 0.7 copy.10.local_ref
  2.7 2.9 %shard_map.85 = (s32[96]{0:T(128)}, f32[96]{0:T(128)}, s32[96]{0:T(128)}, f32[96]{0:T(128)}, s32[32]{0:T(128)}, /*index=5*/f32[32]{0:T(128)}) custom-call(s32[32,3]{1,0:T(8,128)} %copy.9.owner_ref, s32[32,3]{1,0:T(8,128)} %copy.10.local_ref), custom_call_target="tpu_custom_call" | custom-call | tf_op jit(solution)/shard_map/pallas_call | solution.py:567
  5.6 0.0 copy-start.3
  5.6 0.0 copy-start.4
  5.6 0.0 copy-start.5
  5.7 0.0 copy-start
  5.7 0.0 copy-start.1
  5.7 0.0 copy-start.2
  5.7 0.6 copy-done.3
  6.2 0.0 copy-done.4
  6.2 0.0 copy-done.5
  6.3 0.0 copy-done
  6.3 0.0 copy-done.1
  6.3 0.0 copy-done.2
  6.3 178.9 %shard_map.86 = (bf16[128,4096]{1,0:T(8,128)(2,1)S(1)}, bf16[128,4096]{1,0:T(8,128)(2,1)}, bf16[128,4096]{1,0:T(8,128)(2,1)}) custom-call(s32[96]{0:T(128)S(1)} %copy-done, f32[96]{0:T(128)S(1)} %copy-done.1, s32[96]{0:T(128)S(1)} %copy-done.2, f32[96]{0:T(128)S(1)} %copy-done.3, s32[32]{0:T(128)S(1)} %copy-done.4, f32[32]{0:T(128)S(1)} %copy-done.5, ...), custom_call_target="tpu_custom_call" | custom-call | tf_op jit(solution)/shard_map/pallas_call | solution.py:578
  185.3 0.0 copy-start.7
  185.3 1.0 copy.14
  186.2 0.6 copy-done.7
  186.9 0.0 copy-start.6
  186.9 1.0 copy.15
  187.8 0.6 copy-done.6
  188.5 1.0 copy.16
Async XLA Ops:
  0.6 1.4 copy-start.8
  5.6 0.6 copy-start.3
  5.6 0.6 copy-start.4
  5.6 0.6 copy-start.5
  5.7 0.7 copy-start
  5.7 0.6 copy-start.1
  5.7 0.7 copy-start.2
  185.3 1.6 copy-start.7
  186.9 1.6 copy-start.6
where the time goes:
time: 190 us; the launch traced here: 189 us
  Pallas kernels  182 us (96%)
  local copies, waits for them, and re-layouts  6.9 us (4%)
    pallas_call x1, Pallas kernels, one_head(): pl.pallas_call(functools.partial(head_kernel, ctx_size, heads_axis), out_...  179 us
    unnamed x23, local copies, waits for them, and re-layouts  6.9 us

commit v1 on v0

--- a/solution.py
+++ b/solution.py
@@ -255,22 +255,13 @@
     return lax.dot_general(left, right, (((1,), (1,)), ((), ())), preferred_element_type=jnp.float32)
 
 
-def links_kernel(
-    range_blocks, owner_ref, local_ref, named_ref, bias_ref, prev_ref, has_prev_ref, last_ref, has_last_ref
-):
-    blocks, randoms = owner_ref.shape
-
-    def clear(block_id, carry):
-        last_ref[block_id] = 0
-        has_last_ref[block_id] = 0.0
-        return carry
-
-    lax.fori_loop(0, blocks, clear, 0)
-
-    def link(block_id, carry):
+def name_edges(range_blocks, owner_ref, local_ref, named_ref, bias_ref):
+    randoms, blocks = owner_ref.shape
+
+    def name_step(block_id, carry):
         earlier = []
         for nth in range(randoms):
-            named = owner_ref[block_id, nth] * range_blocks + local_ref[block_id, nth]
+            named = owner_ref[nth, block_id] * range_blocks + local_ref[nth, block_id]
             fresh = (named >= GLOBALS) & ((named < block_id - 1) | (named > block_id + 1))
             for before in earlier:
                 fresh = fresh & (named != before)
@@ -278,23 +269,40 @@
             edge = block_id * randoms + nth
             named_ref[edge] = named
             bias_ref[edge] = jnp.where(fresh, 0.0, -NEG_BIG).astype(jnp.float32)
-            prev_ref[edge] = last_ref[named]
-            has_prev_ref[edge] = has_last_ref[named]
-
-            @pl.when(block_id >= GLOBALS)
-            def _():
-                last_ref[named] = edge
-                has_last_ref[named] = 1.0
-
         return carry
 
-    lax.fori_loop(0, blocks, link, 0)
-
-
-def head_kernel(ctx_size, heads_axis, named_ref, bias_ref, prev_ref, has_prev_ref, last_ref, has_last_ref,
-                k_in, v_in, q_in, g_in, dq_out, dk_out, dv_out,
-                kv_ref, qg_ref, grads_ref, acc_ref, edge_ref, kt_ref, pair_ref, s_ref, dp_ref,
-                send_sem, recv_sem, own_sem):
+    lax.fori_loop(0, blocks, name_step, 0)
+
+
+def link_edges(range_blocks, owner, local, width):
+    randoms, blocks = owner.shape
+    named = owner * range_blocks + local
+    row_id = lax.broadcasted_iota(jnp.int32, (blocks, blocks), 0)
+    column_id = lax.broadcasted_iota(jnp.int32, (blocks, blocks), 1)
+    across = [jnp.broadcast_to(named[nth : nth + 1], (blocks, blocks)) for nth in range(randoms)]
+
+    def latest(wanted, before):
+        found = jnp.full((blocks, blocks), -1, jnp.int32)
+        for nth in range(randoms):
+            hit = (across[nth] == wanted) & (column_id >= GLOBALS) & (column_id < before)
+            found = jnp.maximum(found, jnp.where(hit, column_id * randoms + nth, -1))
+        return jnp.max(found, axis=1, keepdims=True)
+
+    columns = []
+    for nth in range(randoms):
+        down = jnp.sum(jnp.where(row_id == column_id, across[nth], 0), axis=1, keepdims=True)
+        columns.append(latest(down, row_id))
+    columns.append(latest(row_id, blocks))
+    slot = lax.broadcasted_iota(jnp.int32, (blocks, width), 1)
+    table = jnp.full((blocks, width), -1, jnp.int32)
+    for nth, column in enumerate(columns):
+        table = jnp.where(slot == nth, column, table)
+    return table
+
+
+def head_kernel(ctx_size, heads_axis, owner_ref, local_ref, owner_rows, local_rows, k_in, v_in, q_in, g_in,
+                dq_out, dk_out, dv_out, named_ref, bias_ref, links_ref, table_ref, kv_ref, qg_ref, grads_ref, acc_ref, edge_ref, kt_ref, pair_ref, s_ref, dp_ref,
+                send_sem, recv_sem, own_sem, table_sem):
     blocks, randoms = kv_ref.shape[0], edge_ref.shape[0] // kv_ref.shape[0]
     devices = ctx_size * heads_axis
     score_scale = 1.0 / math.sqrt(HEAD_DIM)
@@ -306,7 +314,6 @@
     bf16 = jnp.bfloat16
     ctx_id, head_id = lax.axis_index("ctx"), lax.axis_index("head")
     me = ctx_id * heads_axis + head_id
-    own_step = ctx_size - 1
     ins = (k_in, v_in, q_in, g_in)
     landing = (kv_ref, kv_ref, qg_ref, qg_ref)
     outs = (dq_out, dk_out, dv_out)
@@ -314,8 +321,11 @@
     def head_columns(block_id):
         return pl.ds(pl.multiple_of(block_id * HEAD_DIM, HEAD_DIM), HEAD_DIM)
 
-    def peer_at(step):
-        ctx_off, head_off = ctx_size - 1 - step % ctx_size, step // ctx_size
+    inner = (ctx_id > 0) & (ctx_id < ctx_size - 1)
+    near = (1, 0)
+    far = (jnp.where(inner, 3, 2), jnp.where(inner, 2, 3))
+
+    def peer_at(ctx_off, head_off):
         return ctx_id ^ ctx_off, head_id ^ head_off, ctx_off * heads_axis + head_off
 
     def ends(which, peer):
@@ -345,35 +355,46 @@
         src, dst = ends(which, me)
         return pltpu.make_async_copy(src, dst, own_sem.at[which])
 
-    def over_peers(action):
-        def one(step, carry):
-            @pl.when(step != own_step)
-            def _():
-                action(*peer_at(step))
-
+    def over_peers(ctx_offs, action, first=0, until=heads_axis):
+        def one(head_off, carry):
+            for ctx_off in ctx_offs:
+                if isinstance(ctx_off, int) and ctx_off == 0:
+
+                    @pl.when(head_off > 0)
+                    def _():
+                        action(*peer_at(ctx_off, head_off))
+
+                else:
+                    action(*peer_at(ctx_off, head_off))
             return carry
 
-        lax.fori_loop(0, devices, one, 0)
-
-    def start_all(*names):
+        lax.fori_loop(first, until, one, 0)
+
+    def start_all(ctx_offs, *names):
         def action(*peer):
             for which in names:
                 remote(which, *peer).start()
 
-        over_peers(action)
+        over_peers(ctx_offs, action)
 
     barrier = pltpu.get_barrier_semaphore()
 
     def greet(peer_ctx, peer_head, offset):
         pl.semaphore_signal(barrier, inc=1, device_id=(peer_ctx, peer_head), device_id_type=MESH)
 
-    over_peers(greet)
+    over_peers(far + near, greet)
     pl.semaphore_wait(barrier, devices - 1)
-    start_all(0)
-    start_all(1)
-    start_all(2, 3)
+    start_all(far + near, 0)
+    start_all(far + near, 1)
+
     for which in range(4):
         own(which).start()
+    table_ref[...] = link_edges(
+        blocks // ctx_size, owner_rows[...], local_rows[...], table_ref.shape[1]
+    )
+    table_copy = pltpu.make_async_copy(table_ref, links_ref, table_sem)
+    table_copy.start()
+    name_edges(blocks // ctx_size, owner_ref, local_ref, named_ref, bias_ref)
     pair_ref[...] = jnp.zeros_like(pair_ref)
     acc_ref[...] = jnp.zeros_like(acc_ref)
     edge_ref[: GLOBALS * randoms] = jnp.zeros(
@@ -381,12 +402,19 @@
     )
     for which in range(4):
         own(which).wait()
+    table_copy.wait()
+
+    early = 4
 
     def keys_arrived(*peer):
         remote(0, *peer).wait_recv()
         remote(1, *peer).wait_recv()
 
-    over_peers(keys_arrived)
+    over_peers(far, keys_arrived, 0, early)
+
+    start_all(far + near, 2, 3)
+    over_peers(far, keys_arrived, early, heads_axis)
+    over_peers(near, keys_arrived)
 
     def turn_step(block_id, carry):
         kt_ref[block_id] = kv_ref[block_id, :, :HEAD_DIM].T
@@ -436,11 +464,15 @@
             dq_acc += dot_nn(kt_ref[key_id], ds_bf)
         grads_ref[0, block_id] = (dq_acc.T * score_scale).astype(bf16)
 
-    def block_step(step, carry):
-        peer = peer_at(step)
+    def send_queries_grad(*peer):
+        @pl.when(peer[0] * heads_axis + peer[1] >= GLOBALS)
+        def _():
+            remote(4, *peer).start()
+
+    def handle(send, remote_block, *peer):
         block_id = peer[0] * heads_axis + peer[1]
 
-        @pl.when(step != own_step)
+        @pl.when(remote_block)
         def _():
             remote(2, *peer).wait_recv()
             remote(3, *peer).wait_recv()
@@ -449,13 +481,22 @@
         def _():
             attend(block_id)
 
-            @pl.when(step != own_step)
+            @pl.when(send & remote_block)
             def _():
                 remote(4, *peer).start()
 
+    def block_step(step, carry):
+        group_id, head_off = step // heads_axis, step % heads_axis
+        far_off = jnp.where(group_id == 2, far[0], far[1])
+        ctx_off = jnp.where(group_id < 2, group_id, far_off)
+        handle((group_id < 2) | jnp.logical_not(inner), step > 0, *peer_at(ctx_off, head_off))
         return carry
 
     lax.fori_loop(0, devices, block_step, 0)
+
+    @pl.when(inner)
+    def _():
+        over_peers(far, send_queries_grad)
 
     q_glob = qg_ref[:GLOBALS, :, :HEAD_DIM].reshape(glob_rows, HEAD_DIM)
     g_glob = qg_ref[:GLOBALS, :, HEAD_DIM:].reshape(glob_rows, HEAD_DIM)
@@ -519,20 +560,31 @@
 
     own(4).start()
 
-    def chain_step(edge, carry):
-        edge_ref[edge] += has_prev_ref[edge] * edge_ref[prev_ref[edge]]
+    def linked(block_id, slot):
+        edge = links_ref[block_id, slot]
+        weight = jnp.where(edge >= 0, 1.0, 0.0).astype(jnp.float32)
+        return weight * edge_ref[jnp.maximum(edge, 0)]
+
+    def chain_step(block_id, carry):
+        for nth in range(randoms):
+            edge_ref[block_id * randoms + nth] += linked(block_id, nth)
         return carry
 
-    lax.fori_loop(GLOBALS * randoms, blocks * randoms, chain_step, 0)
-
-    def finish_step(step, carry):
-        peer = peer_at(step)
+    lax.fori_loop(GLOBALS, blocks, chain_step, 0)
+
+    def finish(*peer):
         block_id = peer[0] * heads_axis + peer[1]
-        total = acc_ref[block_id] + has_last_ref[block_id] * edge_ref[last_ref[block_id]]
+        total = acc_ref[block_id] + linked(block_id, randoms)
         grads_ref[1, block_id] = (total[:, :HEAD_DIM] * score_scale).astype(bf16)
         grads_ref[2, block_id] = total[:, HEAD_DIM:].astype(bf16)
 
-        @pl.when(step != own_step)
+    def finish_step(step, carry):
+        head_off, turn = step // ctx_size, step % ctx_size
+        ctx_off = jnp.where(turn == 0, far[0], jnp.where(turn == 1, far[1], ctx_size - 1 - turn))
+        peer = peer_at(ctx_off, head_off)
+        finish(*peer)
+
+        @pl.when(step != ctx_size - 1)
         def _():
             remote(5, *peer).start()
             remote(6, *peer).start()
@@ -551,7 +603,12 @@
         for which in range(4, 7):
             remote(which, *peer).wait()
 
-    over_peers(all_done)
+    over_peers(far + near, all_done)
+
+
+def copy_kernel(count, *refs):
+    for nth in range(count):
+        refs[count + nth][...] = refs[nth][...]
 
 
 def one_head(queries, keys_in, values_in, out_grad, rand_owner, rand_local):
@@ -563,54 +620,52 @@
     edges = blocks * randoms
     anywhere = pl.BlockSpec(memory_space=pl.ANY)
     smem = pl.BlockSpec(memory_space=pltpu.SMEM)
+    vmem = pl.BlockSpec(memory_space=pltpu.VMEM)
     bf16 = jnp.bfloat16
-    tables = pl.pallas_call(
-        functools.partial(links_kernel, blocks // ctx_size),
-        out_shape=[
-            jax.ShapeDtypeStruct((count,), kind)
-            for count in (edges, edges, blocks)
-            for kind in (jnp.int32, jnp.float32)
+    grads = pl.pallas_call(
+        functools.partial(head_kernel, ctx_size, heads_axis),
+        out_shape=[jax.ShapeDtypeStruct((rows, feat_width), bf16)] * 3,
+        in_specs=[smem] * 2 + [vmem] * 2 + [anywhere] * 4,
+        out_specs=[anywhere] * 3,
+        scratch_shapes=[
+            pltpu.SMEM((edges,), jnp.int32),
+            pltpu.SMEM((edges,), jnp.float32),
+            pltpu.SMEM((blocks, 128), jnp.int32),
+            pltpu.VMEM((blocks, 128), jnp.int32),
+            pltpu.VMEM((blocks, BLOCK_LEN, 2 * HEAD_DIM), bf16),
+            pltpu.VMEM((blocks, BLOCK_LEN, 2 * HEAD_DIM), bf16),
+            pltpu.VMEM((3, blocks, BLOCK_LEN, HEAD_DIM), bf16),
+            pltpu.VMEM((blocks, BLOCK_LEN, 2 * HEAD_DIM), jnp.float32),
+            pltpu.VMEM((edges, BLOCK_LEN, 2 * HEAD_DIM), jnp.float32),
+            pltpu.VMEM((blocks, HEAD_DIM, BLOCK_LEN), bf16),
+            pltpu.VMEM((2 * BLOCK_LEN, 2 * HEAD_DIM), bf16),
+            pltpu.VMEM((tokens, GLOBALS * BLOCK_LEN), jnp.float32),
+            pltpu.VMEM((tokens, GLOBALS * BLOCK_LEN), jnp.float32),
+            pltpu.SemaphoreType.DMA((7, devices)),
+            pltpu.SemaphoreType.DMA((7, devices)),
+            pltpu.SemaphoreType.DMA((7,)),
+            pltpu.SemaphoreType.DMA,
         ],
-        in_specs=[smem] * 2,
-        out_specs=[smem] * 6,
-    )(rand_owner, rand_local)
+        compiler_params=pltpu.CompilerParams(
+            collective_id=1, has_side_effects=True, vmem_limit_bytes=52 << 20
+        ),
+    )(rand_owner.T, rand_local.T, rand_owner.T, rand_local.T, keys_in, values_in, queries, out_grad)
+    tile = pl.BlockSpec((rows // 4, feat_width), lambda step: (step, 0))
     return tuple(
         pl.pallas_call(
-            functools.partial(head_kernel, ctx_size, heads_axis),
+            functools.partial(copy_kernel, 3),
             out_shape=[jax.ShapeDtypeStruct((rows, feat_width), bf16)] * 3,
-            in_specs=[smem] * 6 + [anywhere] * 4,
-            out_specs=[anywhere] * 3,
-            scratch_shapes=[
-                pltpu.VMEM((blocks, BLOCK_LEN, 2 * HEAD_DIM), bf16),
-                pltpu.VMEM((blocks, BLOCK_LEN, 2 * HEAD_DIM), bf16),
-                pltpu.VMEM((3, blocks, BLOCK_LEN, HEAD_DIM), bf16),
-                pltpu.VMEM((blocks, BLOCK_LEN, 2 * HEAD_DIM), jnp.float32),
-                pltpu.VMEM((edges, BLOCK_LEN, 2 * HEAD_DIM), jnp.float32),
-                pltpu.VMEM((blocks, HEAD_DIM, BLOCK_LEN), bf16),
-                pltpu.VMEM((2 * BLOCK_LEN, 2 * HEAD_DIM), bf16),
-                pltpu.VMEM((tokens, GLOBALS * BLOCK_LEN), jnp.float32),
-                pltpu.VMEM((tokens, GLOBALS * BLOCK_LEN), jnp.float32),
-                pltpu.SemaphoreType.DMA((7, devices)),
-                pltpu.SemaphoreType.DMA((7, devices)),
-                pltpu.SemaphoreType.DMA((7,)),
-            ],
-            compiler_params=pltpu.CompilerParams(
-                collective_id=1, has_side_effects=True, vmem_limit_bytes=52 << 20
-            ),
-        )(
-            *tables,
-            keys_in,
-            values_in,
-            queries,
-            out_grad,
-        )
+            grid=(4,),
+            in_specs=[tile] * 3,
+            out_specs=[tile] * 3,
+        )(*grads)
     )
 
 
 def per_device(*args):
     devices = lax.axis_size(("ctx", "head"))
     rows, feat_width = args[0].shape
-    fits = feat_width == devices * HEAD_DIM and rows == BLOCK_LEN and devices % 4 == 0
+    fits = feat_width == devices * HEAD_DIM and rows == BLOCK_LEN and lax.axis_size("ctx") == 4
     return one_head(*args) if fits else split_heads(*args)
 
 

time: 190 us -> 186 us (0.979)
  the two profiles are of different devices: /device:TPU:0 before, /device:TPU:17 now
where the time goes in v1:
time: 186 us; the launch traced here: 183 us
  Pallas kernels  180 us (97%)
  local copies, waits for them, and re-layouts  2.35 us (1%)
    pallas_call x1, Pallas kernels, one_head(): pl.pallas_call(functools.partial(head_kernel, ctx_size, heads_axis), out_...  176 us
    pallas_call x1, Pallas kernels, one_head(): pl.pallas_call(functools.partial(copy_kernel, 3), out_shape=[jax.ShapeDty...  4.12 us

profile of v1, /device:TPU:17, one launch (start us, length us, event | category | flops | bytes accessed | tf_op | source)
XLA Modules:
  0.0 182.7 jit_solution(13187986299629036546)
XLA Ops:
  0.6 0.0 copy-start.1
  0.6 0.7 copy-done.1
  1.3 0.0 copy-start.2
  1.3 0.7 copy-done.2
  2.0 175.5 %shard_map.85 = (bf16[128,4096]{1,0:T(8,128)(2,1)S(1)}, bf16[128,4096]{1,0:T(8,128)(2,1)}, bf16[128,4096]{1,0:T(8,128)(2,1)}) custom-call(s32[3,32]{1,0:T(4,128)S(1)} %bitcast.2, s32[3,32]{1,0:T(4,128)S(1)} %bitcast.4, s32[3,32]{1,0:T(4,128)S(1)} %bitcast.3, s32[3,32]{1,0:T(4,128)S(1)} %bitcast.5, bf16[128,4096]{1,0:T(8,128)(2,1)} %k_in.1, ...), custom_call_target="tpu_custom_call" | custom-call | tf_op jit(solution)/shard_map/pallas_call | solution.py:625
  177.5 0.0 copy-start
  177.5 1.0 copy-done
  178.5 4.1 %shard_map.86 = (bf16[128,4096]{1,0:T(8,128)(2,1)}, bf16[128,4096]{1,0:T(8,128)(2,1)}, bf16[128,4096]{1,0:T(8,128)(2,1)}) custom-call(bf16[128,4096]{1,0:T(8,128)(2,1)} %copy-done, bf16[128,4096]{1,0:T(8,128)(2,1)} %get-tuple-element.7.refs_1_, bf16[128,4096]{1,0:T(8,128)(2,1)} %get-tuple-element.8.refs_2_), custom_call_target="tpu_custom_call" | custom-call | tf_op jit(solution)/shard_map/pallas_call | solution.py:655
Async XLA Ops:
  0.6 0.7 copy-start.1
  1.3 0.7 copy-start.2
  177.5 1.0 copy-start

commit v2 on v1

--- a/solution.py
+++ b/solution.py
@@ -300,9 +300,10 @@
     return table
 
 
-def head_kernel(ctx_size, heads_axis, owner_ref, local_ref, owner_rows, local_rows, k_in, v_in, q_in, g_in,
-                dq_out, dk_out, dv_out, named_ref, bias_ref, links_ref, table_ref, kv_ref, qg_ref, grads_ref, acc_ref, edge_ref, kt_ref, pair_ref, s_ref, dp_ref,
-                send_sem, recv_sem, own_sem, table_sem):
+def head_kernel(ctx_size, heads_axis, owner_in, local_in, k_in, v_in, q_in, g_in,
+                dq_out, dk_out, dv_out, owner_ref, local_ref, owner_rows, local_rows,
+                named_ref, bias_ref, links_ref, table_ref, kv_ref, qg_ref, grads_ref, acc_ref, edge_ref, kt_ref, pair_ref, s_ref, dp_ref,
+                send_sem, recv_sem, own_sem, table_sem, index_sem):
     blocks, randoms = kv_ref.shape[0], edge_ref.shape[0] // kv_ref.shape[0]
     devices = ctx_size * heads_axis
     score_scale = 1.0 / math.sqrt(HEAD_DIM)
@@ -389,6 +390,16 @@
 
     for which in range(4):
         own(which).start()
+    index_copies = [
+        pltpu.make_async_copy(src, dst, index_sem.at[nth])
+        for nth, (src, dst) in enumerate(
+            zip((owner_in, local_in) * 2, (owner_ref, local_ref, owner_rows, local_rows))
+        )
+    ]
+    for copy in index_copies:
+        copy.start()
+    for copy in index_copies:
+        copy.wait()
     table_ref[...] = link_edges(
         blocks // ctx_size, owner_rows[...], local_rows[...], table_ref.shape[1]
     )
@@ -461,7 +472,15 @@
                 acc_ref[key_id] += dot_nn(left, pair)
             else:
                 edge_ref[block_id * randoms + nth - fixed] = dot_nn(left, pair)
-            dq_acc += dot_nn(kt_ref[key_id], ds_bf)
+            if nth % 2 == 0:
+                waiting, waiting_id = ds_bf, key_id
+            else:
+                dq_acc += dot_nn(
+                    jnp.concatenate([kt_ref[waiting_id], kt_ref[key_id]], axis=1),
+                    jnp.concatenate([waiting, ds_bf], axis=0),
+                )
+        if len(ids) % 2:
+            dq_acc += dot_nn(kt_ref[waiting_id], waiting)
         grads_ref[0, block_id] = (dq_acc.T * score_scale).astype(bf16)
 
     def send_queries_grad(*peer):
@@ -489,14 +508,11 @@
         group_id, head_off = step // heads_axis, step % heads_axis
         far_off = jnp.where(group_id == 2, far[0], far[1])
         ctx_off = jnp.where(group_id < 2, group_id, far_off)
-        handle((group_id < 2) | jnp.logical_not(inner), step > 0, *peer_at(ctx_off, head_off))
+        handle(group_id >= 0, step > 0, *peer_at(ctx_off, head_off))
         return carry
 
     lax.fori_loop(0, devices, block_step, 0)
 
-    @pl.when(inner)
-    def _():
-        over_peers(far, send_queries_grad)
 
     q_glob = qg_ref[:GLOBALS, :, :HEAD_DIM].reshape(glob_rows, HEAD_DIM)
     g_glob = qg_ref[:GLOBALS, :, HEAD_DIM:].reshape(glob_rows, HEAD_DIM)
@@ -607,8 +623,12 @@
 
 
 def copy_kernel(count, *refs):
-    for nth in range(count):
-        refs[count + nth][...] = refs[nth][...]
+    ins, outs, sems = refs[:count], refs[count : 2 * count], refs[2 * count]
+    copies = [pltpu.make_async_copy(ins[nth], outs[nth], sems.at[nth]) for nth in range(count)]
+    for copy in copies:
+        copy.start()
+    for copy in copies:
+        copy.wait()
 
 
 def one_head(queries, keys_in, values_in, out_grad, rand_owner, rand_local):
@@ -619,15 +639,19 @@
     blocks, randoms = rand_owner.shape
     edges = blocks * randoms
     anywhere = pl.BlockSpec(memory_space=pl.ANY)
-    smem = pl.BlockSpec(memory_space=pltpu.SMEM)
     vmem = pl.BlockSpec(memory_space=pltpu.VMEM)
+    hbm = pl.BlockSpec(memory_space=pltpu.HBM)
     bf16 = jnp.bfloat16
     grads = pl.pallas_call(
         functools.partial(head_kernel, ctx_size, heads_axis),
         out_shape=[jax.ShapeDtypeStruct((rows, feat_width), bf16)] * 3,
-        in_specs=[smem] * 2 + [vmem] * 2 + [anywhere] * 4,
-        out_specs=[anywhere] * 3,
+        in_specs=[hbm] * 6,
+        out_specs=[vmem] * 3,
         scratch_shapes=[
+            pltpu.SMEM((randoms, blocks), jnp.int32),
+            pltpu.SMEM((randoms, blocks), jnp.int32),
+            pltpu.VMEM((randoms, blocks), jnp.int32),
+            pltpu.VMEM((randoms, blocks), jnp.int32),
             pltpu.SMEM((edges,), jnp.int32),
             pltpu.SMEM((edges,), jnp.float32),
             pltpu.SMEM((blocks, 128), jnp.int32),
@@ -645,19 +669,20 @@
             pltpu.SemaphoreType.DMA((7, devices)),
             pltpu.SemaphoreType.DMA((7,)),
             pltpu.SemaphoreType.DMA,
+            pltpu.SemaphoreType.DMA((4,)),
         ],
         compiler_params=pltpu.CompilerParams(
-            collective_id=1, has_side_effects=True, vmem_limit_bytes=52 << 20
+            collective_id=1, has_side_effects=True, vmem_limit_bytes=50 << 20
         ),
-    )(rand_owner.T, rand_local.T, rand_owner.T, rand_local.T, keys_in, values_in, queries, out_grad)
-    tile = pl.BlockSpec((rows // 4, feat_width), lambda step: (step, 0))
+    )(rand_owner.T, rand_local.T, keys_in, values_in, queries, out_grad)
     return tuple(
         pl.pallas_call(
             functools.partial(copy_kernel, 3),
             out_shape=[jax.ShapeDtypeStruct((rows, feat_width), bf16)] * 3,
-            grid=(4,),
-            in_specs=[tile] * 3,
-            out_specs=[tile] * 3,
+            in_specs=[vmem] * 3,
+            out_specs=[anywhere] * 3,
+            scratch_shapes=[pltpu.SemaphoreType.DMA((3,))],
+            compiler_params=pltpu.CompilerParams(vmem_limit_bytes=4 << 20),
         )(*grads)
     )
 

time: 186 us -> 178 us (0.957)
  Pallas kernels: 180 us -> 172 us
    pallas_call x1, Pallas kernels: 176 us -> 171 us  [one_head(): pl.pallas_call(functools.partial(head_kernel, ctx_size, heads_axis), out_...]
    pallas_call x1, Pallas kernels: 4.12 us -> 1.69 us  [one_head(): pl.pallas_call(functools.partial(copy_kernel, 3), out_shape=[jax.ShapeDty...]
where the time goes in v2:
time: 178 us; the launch traced here: 174 us
  Pallas kernels  172 us (97%)
    pallas_call x1, Pallas kernels, one_head(): pl.pallas_call(functools.partial(head_kernel, ctx_size, heads_axis), out_...  171 us

profile of v2, /device:TPU:17, one launch (start us, length us, event | category | flops | bytes accessed | tf_op | source)
XLA Modules:
  0.0 174.3 jit_solution(15800809702136117423)
XLA Ops:
  0.6 0.0 copy-start
  0.6 0.7 copy-done
  1.3 0.0 copy-start.1
  1.3 0.7 copy-done.1
  2.0 170.6 %shard_map.85 = (bf16[128,4096]{1,0:T(8,128)(2,1)S(1)}, bf16[128,4096]{1,0:T(8,128)(2,1)S(1)}, bf16[128,4096]{1,0:T(8,128)(2,1)S(1)}) custom-call(s32[3,32]{1,0:T(4,128)S(1)} %bitcast.2, s32[3,32]{1,0:T(4,128)S(1)} %bitcast.3, bf16[128,4096]{1,0:T(8,128)(2,1)} %k_in.1, bf16[128,4096]{1,0:T(8,128)(2,1)} %v_in.1, bf16[128,4096]{1,0:T(8,128)(2,1)} %q_in.1, ...), custom_call_target="tpu_custom_call" | custom-call | tf_op jit(solution)/shard_map/pallas_call | solution.py:645
  172.6 1.7 shard_map.86
Async XLA Ops:
  0.6 0.7 copy-start
  1.3 0.7 copy-start.1

commit v3 on v2

--- a/solution.py
+++ b/solution.py
@@ -387,6 +387,7 @@
     pl.semaphore_wait(barrier, devices - 1)
     start_all(far + near, 0)
     start_all(far + near, 1)
+    start_all(far + near, 2, 3)
 
     for which in range(4):
         own(which).start()
@@ -415,17 +416,11 @@
         own(which).wait()
     table_copy.wait()
 
-    early = 4
-
     def keys_arrived(*peer):
         remote(0, *peer).wait_recv()
         remote(1, *peer).wait_recv()
 
-    over_peers(far, keys_arrived, 0, early)
-
-    start_all(far + near, 2, 3)
-    over_peers(far, keys_arrived, early, heads_axis)
-    over_peers(near, keys_arrived)
+    over_peers(far + near, keys_arrived)
 
     def turn_step(block_id, carry):
         kt_ref[block_id] = kv_ref[block_id, :, :HEAD_DIM].T
@@ -613,13 +608,16 @@
     for which in range(4, 7):
         own(which).wait()
 
-    def all_done(*peer):
-        for which in range(4):
+    def all_sent(*peer):
+        for which in range(7):
             remote(which, *peer).wait_send()
+
+    def all_here(*peer):
         for which in range(4, 7):
-            remote(which, *peer).wait()
-
-    over_peers(far + near, all_done)
+            remote(which, *peer).wait_recv()
+
+    over_peers(far + near, all_sent)
+    over_peers(near + far, all_here)
 
 
 def copy_kernel(count, *refs):
@@ -642,6 +640,7 @@
     vmem = pl.BlockSpec(memory_space=pltpu.VMEM)
     hbm = pl.BlockSpec(memory_space=pltpu.HBM)
     bf16 = jnp.bfloat16
+    index_arrays = [pltpu.with_memory_space_constraint(index.T, pltpu.HBM) for index in (rand_owner, rand_local)]
     grads = pl.pallas_call(
         functools.partial(head_kernel, ctx_size, heads_axis),
         out_shape=[jax.ShapeDtypeStruct((rows, feat_width), bf16)] * 3,
@@ -674,7 +673,7 @@
         compiler_params=pltpu.CompilerParams(
             collective_id=1, has_side_effects=True, vmem_limit_bytes=50 << 20
         ),
-    )(rand_owner.T, rand_local.T, keys_in, values_in, queries, out_grad)
+    )(*index_arrays, keys_in, values_in, queries, out_grad)
     return tuple(
         pl.pallas_call(
             functools.partial(copy_kernel, 3),

time: 178 us -> 174 us (0.978)
  Pallas kernels: 172 us -> 170 us
    pallas_call x1, Pallas kernels: 171 us -> 169 us  [one_head(): pl.pallas_call(functools.partial(head_kernel, ctx_size, heads_axis), out_...]
where the time goes in v3:
time: 174 us; the launch traced here: 171 us
  Pallas kernels  170 us (98%)
    pallas_call x1, Pallas kernels, one_head(): pl.pallas_call(functools.partial(head_kernel, ctx_size, heads_axis), out_...  169 us

profile of v3, /device:TPU:17, one launch (start us, length us, event | category | flops | bytes accessed | tf_op | source)
XLA Modules:
  0.0 170.9 jit_solution(17919524034756967951)
XLA Ops:
  0.6 168.6 %shard_map.85 = (bf16[128,4096]{1,0:T(8,128)(2,1)S(1)}, bf16[128,4096]{1,0:T(8,128)(2,1)S(1)}, bf16[128,4096]{1,0:T(8,128)(2,1)S(1)}) custom-call(s32[3,32]{1,0:T(4,128)} %bitcast.2, s32[3,32]{1,0:T(4,128)} %bitcast.3, bf16[128,4096]{1,0:T(8,128)(2,1)} %k_in.1, bf16[128,4096]{1,0:T(8,128)(2,1)} %v_in.1, bf16[128,4096]{1,0:T(8,128)(2,1)} %q_in.1, ...), custom_call_target="tpu_custom_call" | custom-call | tf_op jit(solution)/shard_map/pallas_call | solution.py:644
  169.2 1.7 shard_map.86

commit v4 on v3

--- a/solution.py
+++ b/solution.py
@@ -357,7 +357,8 @@
         return pltpu.make_async_copy(src, dst, own_sem.at[which])
 
     def over_peers(ctx_offs, action, first=0, until=heads_axis):
-        def one(head_off, carry):
+        def one(turn, carry):
+            head_off = turn ^ (ctx_id % 2)
             for ctx_off in ctx_offs:
                 if isinstance(ctx_off, int) and ctx_off == 0:
 
@@ -591,7 +592,7 @@
 
     def finish_step(step, carry):
         head_off, turn = step // ctx_size, step % ctx_size
-        ctx_off = jnp.where(turn == 0, far[0], jnp.where(turn == 1, far[1], ctx_size - 1 - turn))
+        ctx_off = jnp.where(turn == 0, far[1], jnp.where(turn == 1, far[0], ctx_size - 1 - turn))
         peer = peer_at(ctx_off, head_off)
         finish(*peer)
 

time: 174 us -> 173 us (level); the launches traced: 171 us -> 172 us
  no operation moved by 1% of the time
where the time goes in v4:
time: 173 us; the launch traced here: 172 us
  Pallas kernels  171 us (99%)
    pallas_call x1, Pallas kernels, one_head(): pl.pallas_call(functools.partial(head_kernel, ctx_size, heads_axis), out_...  170 us

profile of v4, /device:TPU:17, one launch (start us, length us, event | category | flops | bytes accessed | tf_op | source)
XLA Modules:
  0.0 172.1 jit_solution(813649596285715280)
XLA Ops:
  0.6 169.8 %shard_map.85 = (bf16[128,4096]{1,0:T(8,128)(2,1)S(1)}, bf16[128,4096]{1,0:T(8,128)(2,1)S(1)}, bf16[128,4096]{1,0:T(8,128)(2,1)S(1)}) custom-call(s32[3,32]{1,0:T(4,128)} %bitcast.2, s32[3,32]{1,0:T(4,128)} %bitcast.3, bf16[128,4096]{1,0:T(8,128)(2,1)} %k_in.1, bf16[128,4096]{1,0:T(8,128)(2,1)} %v_in.1, bf16[128,4096]{1,0:T(8,128)(2,1)} %q_in.1, ...), custom_call_target="tpu_custom_call" | custom-call | tf_op jit(solution)/shard_map/pallas_call | solution.py:645
  170.4 1.7 shard_map.86

commit v5 on v4

--- a/solution.py
+++ b/solution.py
@@ -591,12 +591,12 @@
         grads_ref[2, block_id] = total[:, HEAD_DIM:].astype(bf16)
 
     def finish_step(step, carry):
-        head_off, turn = step // ctx_size, step % ctx_size
-        ctx_off = jnp.where(turn == 0, far[1], jnp.where(turn == 1, far[0], ctx_size - 1 - turn))
+        head_off, turn = step % heads_axis, step // heads_axis
+        ctx_off = jnp.where(turn == 0, 2, jnp.where(turn == 1, 3, ctx_size - 1 - turn))
         peer = peer_at(ctx_off, head_off)
         finish(*peer)
 
-        @pl.when(step != ctx_size - 1)
+        @pl.when((head_off > 0) | (turn < ctx_size - 1))
         def _():
             remote(5, *peer).start()
             remote(6, *peer).start()

time: 173 us -> 172 us (level)
  no operation moved by 1% of the time
where the time goes in v5:
time: 172 us
  Pallas kernels  171 us (99%)
    pallas_call x1, Pallas kernels, one_head(): pl.pallas_call(functools.partial(head_kernel, ctx_size, heads_axis), out_...  170 us

profile of v5, /device:TPU:17, one launch (start us, length us, event | category | flops | bytes accessed | tf_op | source)
XLA Modules:
  0.0 172.1 jit_solution(3669808694375345064)
XLA Ops:
  0.6 169.7 %shard_map.85 = (bf16[128,4096]{1,0:T(8,128)(2,1)S(1)}, bf16[128,4096]{1,0:T(8,128)(2,1)S(1)}, bf16[128,4096]{1,0:T(8,128)(2,1)S(1)}) custom-call(s32[3,32]{1,0:T(4,128)} %bitcast.2, s32[3,32]{1,0:T(4,128)} %bitcast.3, bf16[128,4096]{1,0:T(8,128)(2,1)} %k_in.1, bf16[128,4096]{1,0:T(8,128)(2,1)} %v_in.1, bf16[128,4096]{1,0:T(8,128)(2,1)} %q_in.1, ...), custom_call_target="tpu_custom_call" | custom-call | tf_op jit(solution)/shard_map/pallas_call | solution.py:645
  170.4 1.7 shard_map.86

commit v6 on v5

--- a/solution.py
+++ b/solution.py
@@ -593,10 +593,10 @@
     def finish_step(step, carry):
         head_off, turn = step % heads_axis, step // heads_axis
         ctx_off = jnp.where(turn == 0, 2, jnp.where(turn == 1, 3, ctx_size - 1 - turn))
-        peer = peer_at(ctx_off, head_off)
+        peer = peer_at(ctx_off, head_off ^ (ctx_id % 2))
         finish(*peer)
 
-        @pl.when((head_off > 0) | (turn < ctx_size - 1))
+        @pl.when(peer[2] > 0)
         def _():
             remote(5, *peer).start()
             remote(6, *peer).start()

time: 172 us -> 172 us (level)
  no operation moved by 1% of the time
where the time goes in v6:
time: 172 us
  Pallas kernels  171 us (99%)
    pallas_call x1, Pallas kernels, one_head(): pl.pallas_call(functools.partial(head_kernel, ctx_size, heads_axis), out_...  170 us

profile of v6, /device:TPU:17, one launch (start us, length us, event | category | flops | bytes accessed | tf_op | source)
XLA Modules:
  0.0 172.1 jit_solution(962474662560417166)
XLA Ops:
  0.6 169.7 %shard_map.85 = (bf16[128,4096]{1,0:T(8,128)(2,1)S(1)}, bf16[128,4096]{1,0:T(8,128)(2,1)S(1)}, bf16[128,4096]{1,0:T(8,128)(2,1)S(1)}) custom-call(s32[3,32]{1,0:T(4,128)} %bitcast.2, s32[3,32]{1,0:T(4,128)} %bitcast.3, bf16[128,4096]{1,0:T(8,128)(2,1)} %k_in.1, bf16[128,4096]{1,0:T(8,128)(2,1)} %v_in.1, bf16[128,4096]{1,0:T(8,128)(2,1)} %q_in.1, ...), custom_call_target="tpu_custom_call" | custom-call | tf_op jit(solution)/shard_map/pallas_call | solution.py:645
  170.4 1.7 shard_map.86
